TPU v7x, 256 devices: a whole 4x4x8 slice. The times are simulated.
256 devices in a mesh: ctx: 64 (over z, x, core), head: 4 (over y).
Axes of the slice: x: 4, y: 4, z: 8, core: 2. Of those that a mesh axis runs over, the one named last changes fastest.
Arguments:
- queries: bfloat16 [8192, 4096], P('ctx', 'head'), may hold values from -40 to 40
- keys: bfloat16 [8192, 4096], P('ctx', 'head'), may hold values from -40 to 40
- values: bfloat16 [8192, 4096], P('ctx', 'head'), may hold values from -50 to 50
- pattern: int32 [64, 8], replicated, may hold values from -1 to 63, as said below
- upstream: bfloat16 [8192, 4096], P('ctx', 'head'), may hold values from -6 to 6
Outputs:
- normed: bfloat16 [8192, 4096], P('ctx', 'head')
- grad_queries: bfloat16 [8192, 4096], P('ctx', 'head')
- grad_keys: bfloat16 [8192, 4096], P('ctx', 'head')
- grad_values: bfloat16 [8192, 4096], P('ctx', 'head')
Inputs may be any that keep to these rules, and one draw needn't show every extreme that they name: `pattern`: entry [i, k] for k < 7 is either i - 2^k or -1, and always -1 where i < 2^k; entry [i, 7] is i.
All inputs are finite; a program needn't handle non-finite values.
Results may differ from a plain program's by a relative error of at most 0.04.
Values may be sent and summed in bfloat16 or wider, within the bound.
A program may use at most 64 MiB of HBM per device.

v0:
```python
import jax
import jax.numpy as jnp
from jax import lax
from jax.sharding import PartitionSpec as P

HD = 128
BLOCK = 128
LEVELS = 7
WIDTH = 4096


NEG_BIG = -1e30
EPSILON = 1e-06


def shifted(block, axis, distance):
    devices = range(lax.axis_size(axis))
    route = [(i - distance, i) for i in devices if i - distance in devices]
    return lax.ppermute(block, axis, route)


def for_sending(x):
    return jax.tree.map(lambda a: a.astype(jnp.bfloat16) if a.dtype == jnp.float32 else a, x)


def route_table(blocks, levels):
    routing = []
    for query_block in range(blocks):
        for level_index in range(levels + 1):
            if level_index == levels:
                routing.append((0, query_block))
            else:
                distance = 2**level_index
                routing.append(
                    (-((query_block - distance) // blocks), (query_block - distance) % blocks)
                )
    return routing


def pair_grads(
    query_tiles, grad_tiles, lse_tiles, delta_tiles, key_tiles, value_tiles, keep_mask, score_scale
):
    scores = (
        jnp.einsum("pqhd,pkhd->phqk", query_tiles, key_tiles, preferred_element_type=jnp.float32)
        * score_scale
    )
    scores = jnp.where(keep_mask[:, None], scores, NEG_BIG)
    weights = jnp.exp(scores - lse_tiles[..., None])
    prob_tiles = weights.astype(jnp.bfloat16)
    grad_probs = jnp.einsum(
        "pqhd,pkhd->phqk", grad_tiles, value_tiles, preferred_element_type=jnp.float32
    )
    dscore = (weights * (grad_probs - delta_tiles[..., None]) * score_scale).astype(jnp.bfloat16)
    return (dscore, prob_tiles)


def key_grads(dscore, prob_tiles, query_tiles, grad_tiles):
    key_part = jnp.einsum(
        "phqk,pqhd->pkhd", dscore, query_tiles, preferred_element_type=jnp.float32
    )
    value_part = jnp.einsum(
        "phqk,pqhd->pkhd", prob_tiles, grad_tiles, preferred_element_type=jnp.float32
    )
    return jnp.stack((key_part, value_part))


def collect(partials, targets, blocks):
    pieces = []
    for key_index in range(blocks):
        summed = jnp.zeros((2,) + partials.shape[2:], jnp.float32)
        for row_index, target in enumerate(targets):
            if target == key_index:
                summed = summed + partials[:, row_index]
        pieces.append(summed)
    return jnp.stack(pieces, axis=1)


def shards(queries, keys, values, pattern, upstream):
    tokens_here = queries.shape[0]
    heads_here = queries.shape[1] // HD
    blocks = tokens_here // BLOCK
    slot_count = LEVELS + 1
    pair_count = blocks * slot_count
    score_scale = HD ** (-0.5)
    ctx_count = lax.axis_size("ctx")
    device_index = lax.axis_index("ctx")
    routing = route_table(blocks, LEVELS)
    offsets = sorted(
        set((route_entry[0] for route_entry in routing if 0 < route_entry[0] < ctx_count))
    )
    tile_shape = (blocks, BLOCK, heads_here, HD)
    query_blocks = queries.reshape(tile_shape)
    own_pairs = jnp.stack((keys, values)).reshape((2,) + tile_shape)
    sources = {0: own_pairs}
    for offset in offsets:
        fetched = shifted(jnp.stack((keys, values)), "ctx", offset)
        sources[offset] = fetched.reshape((2,) + tile_shape)
    empty_tile = jnp.zeros((2, BLOCK, heads_here, HD), jnp.bfloat16)
    gathered = []
    for source, key_index in routing:
        if source in sources:
            gathered.append(sources[source][:, key_index])
        else:
            gathered.append(empty_tile)
    pair_kv = jnp.stack(gathered, axis=1)
    key_tiles = pair_kv[0]
    value_tiles = pair_kv[1]
    key_stack = key_tiles.reshape((blocks, slot_count) + tile_shape[1:])
    value_stack = value_tiles.reshape((blocks, slot_count) + tile_shape[1:])
    own_rows = lax.dynamic_slice_in_dim(pattern, device_index * blocks, blocks, 0)
    positions = jnp.arange(BLOCK)
    causal = positions[None, :] <= positions[:, None]
    self_slot = jnp.arange(slot_count) == LEVELS
    tile_keep = (own_rows >= 0)[:, :, None, None] & (
        jnp.logical_not(self_slot)[None, :, None, None] | causal[None, None]
    )
    scores = (
        jnp.einsum("bqhd,bskhd->bhqsk", query_blocks, key_stack, preferred_element_type=jnp.float32)
        * score_scale
    )
    scores = jnp.where(jnp.transpose(tile_keep, (0, 2, 1, 3))[:, None], scores, NEG_BIG)
    highest = jnp.max(scores, axis=(3, 4))
    log_total = highest + jnp.log(jnp.sum(jnp.exp(scores - highest[..., None, None]), axis=(3, 4)))
    prob_stack = jnp.exp(scores - log_total[..., None, None]).astype(jnp.bfloat16)
    attention = jnp.einsum(
        "bhqsk,bskhd->bqhd", prob_stack, value_stack, preferred_element_type=jnp.float32
    ).astype(jnp.bfloat16)
    attn_wide = attention.reshape(tokens_here, heads_here * HD).astype(jnp.float32)
    square_sum = lax.psum(jnp.sum(attn_wide * attn_wide, axis=1), "head")
    inverse = lax.rsqrt(square_sum / WIDTH + EPSILON)
    normed = (attn_wide * inverse[:, None]).astype(jnp.bfloat16)
    upstream_wide = upstream.astype(jnp.float32)
    cross_term = lax.psum(jnp.sum(upstream_wide * attn_wide, axis=1), "head")
    grad_attn = (
        inverse[:, None] * upstream_wide - attn_wide * (inverse**3 * cross_term / WIDTH)[:, None]
    ).astype(jnp.bfloat16)
    row_delta = jnp.sum(
        (grad_attn.astype(jnp.float32) * attn_wide).reshape(tokens_here, heads_here, HD), axis=2
    )
    row_delta = jnp.transpose(row_delta.reshape(blocks, BLOCK, heads_here), (0, 2, 1))

    def spread(array):
        return jnp.broadcast_to(array[:, None], (blocks, slot_count) + array.shape[1:]).reshape(
            (pair_count,) + array.shape[1:]
        )

    grad_blocks = grad_attn.reshape(tile_shape)
    query_pairs = spread(query_blocks)
    grad_pairs = spread(grad_blocks)
    keep_pairs = tile_keep.reshape(pair_count, BLOCK, BLOCK)
    dscore, prob_pairs = pair_grads(
        query_pairs,
        grad_pairs,
        spread(log_total),
        spread(row_delta),
        key_tiles,
        value_tiles,
        keep_pairs,
        score_scale,
    )
    grad_query = jnp.einsum(
        "phqk,pkhd->pqhd", dscore, key_tiles, preferred_element_type=jnp.float32
    )
    grad_query = jnp.sum(grad_query.reshape((blocks, slot_count) + tile_shape[1:]), axis=1)
    grad_queries = grad_query.astype(jnp.bfloat16).reshape(tokens_here, heads_here * HD)
    local_rows = [row_index for row_index in range(pair_count) if routing[row_index][0] == 0]
    chosen = jnp.array(local_rows, jnp.int32)
    local_terms = key_grads(
        dscore[chosen], prob_pairs[chosen], query_pairs[chosen], grad_pairs[chosen]
    )
    key_sum = collect(local_terms, [routing[row_index][1] for row_index in local_rows], blocks)
    for offset in offsets:
        remote_rows = [
            row_index for row_index in range(pair_count) if routing[row_index][0] == offset
        ]
        chosen = jnp.array(remote_rows, jnp.int32)
        remote_terms = key_grads(
            dscore[chosen], prob_pairs[chosen], query_pairs[chosen], grad_pairs[chosen]
        )
        outgoing = collect(
            remote_terms, [routing[row_index][1] for row_index in remote_rows], blocks
        )
        key_sum = key_sum + shifted(for_sending(outgoing), "ctx", -offset).astype(outgoing.dtype)
    grad_keys = key_sum[0].astype(jnp.bfloat16).reshape(tokens_here, heads_here * HD)
    grad_values = key_sum[1].astype(jnp.bfloat16).reshape(tokens_here, heads_here * HD)
    return (normed, grad_queries, grad_keys, grad_values)


def solution(mesh):
    return jax.shard_map(
        shards,
        mesh=mesh,
        in_specs=(P("ctx", "head"), P("ctx", "head"), P("ctx", "head"), P(), P("ctx", "head")),
        out_specs=(P("ctx", "head"), P("ctx", "head"), P("ctx", "head"), P("ctx", "head")),
        check_vma=False,
    )
```

profile of v0, /device:TPU:64, one launch (start us, length us, event | category | flops | bytes accessed | tf_op | source)
XLA Modules:
  0.0 228.5 jit_solution(5779457081914570927)
XLA Ops:
  3.0 8.1 %collective-permute-start.5 = (bf16[2,128,1024]{1,2,0:T(8,128)(2,1)S(1)}, bf16[2,128,1024]{1,2,0:T(8,128)(2,1)}, u32[]{:S(2)}, u32[]{:S(2)}) collective-permute-start(bf16[2,128,1024]{1,2,0:T(8,128)(2,1)S(1)} %pad_maximum_fusion), channel_id=1, source_target_pairs={{0,128},{4,132},{8,136},{12,140},{16,144},{20,148},{24,152},{28,15... | collective-permute-start | bytes 1572872 | tf_op jit(solution)/shard_map/ppermute | solution.py:19
  11.1 1.9 collective-permute-start.4
  13.0 2.9 %collective-permute-start.3 = (bf16[2,128,1024]{1,2,0:T(8,128)(2,1)S(1)}, bf16[2,128,1024]{1,2,0:T(8,128)(2,1)S(1)}, u32[]{:S(2)}, u32[]{:S(2)}) collective-permute-start(bf16[2,128,1024]{1,2,0:T(8,128)(2,1)S(1)} %pad_maximum_fusion), channel_id=1, source_target_pairs={{0,32},{4,36},{8,40},{12,44},{16,48},{20,52},{24,56},{28,60},{32,6... | collective-permute-start | bytes 1572872 | tf_op jit(solution)/shard_map/ppermute | solution.py:19
  15.9 4.9 %collective-permute-start.2 = (bf16[2,128,1024]{1,2,0:T(8,128)(2,1)S(1)}, bf16[2,128,1024]{1,2,0:T(8,128)(2,1)S(1)}, u32[]{:S(2)}, u32[]{:S(2)}) collective-permute-start(bf16[2,128,1024]{1,2,0:T(8,128)(2,1)S(1)} %pad_maximum_fusion), channel_id=1, source_target_pairs={{0,16},{4,20},{8,24},{12,28},{16,32},{20,36},{24,40},{28,44},{32,4... | collective-permute-start | bytes 1572872 | tf_op jit(solution)/shard_map/ppermute | solution.py:19
  20.9 2.5 %collective-permute-start.1 = (bf16[2,128,1024]{1,2,0:T(8,128)(2,1)S(1)}, bf16[2,128,1024]{1,2,0:T(8,128)(2,1)S(1)}, u32[]{:S(2)}, u32[]{:S(2)}) collective-permute-start(bf16[2,128,1024]{1,2,0:T(8,128)(2,1)S(1)} %pad_maximum_fusion), channel_id=1, source_target_pairs={{0,8},{4,12},{8,16},{12,20},{16,24},{20,28},{24,32},{28,36},{32,40... | collective-permute-start | bytes 1572872 | tf_op jit(solution)/shard_map/ppermute | solution.py:19
  24.3 10.3 %collective-permute-done.5 = bf16[2,128,1024]{1,2,0:T(8,128)(2,1)} collective-permute-done((bf16[2,128,1024]{1,2,0:T(8,128)(2,1)S(1)}, bf16[2,128,1024]{1,2,0:T(8,128)(2,1)}, u32[]{:S(2)}, u32[]{:S(2)}) %collective-permute-start.5) | collective-permute-done | bytes 524320 | tf_op jit(solution)/shard_map/ppermute | solution.py:19
  34.7 1.9 collective-permute-start
  44.5 11.9 %collective-permute-done.4 = bf16[2,128,1024]{1,2,0:T(8,128)(2,1)S(1)} collective-permute-done((bf16[2,128,1024]{1,2,0:T(8,128)(2,1)S(1)}, bf16[2,128,1024]{1,2,0:T(8,128)(2,1)S(1)}, u32[]{:S(2)}, u32[]{:S(2)}) %collective-permute-start.4) | collective-permute-done | bytes 524320 | tf_op jit(solution)/shard_map/ppermute | solution.py:19
  58.4 8.1 %collective-permute-done.3 = bf16[2,128,1024]{1,2,0:T(8,128)(2,1)S(1)} collective-permute-done((bf16[2,128,1024]{1,2,0:T(8,128)(2,1)S(1)}, bf16[2,128,1024]{1,2,0:T(8,128)(2,1)S(1)}, u32[]{:S(2)}, u32[]{:S(2)}) %collective-permute-start.3) | collective-permute-done | bytes 524320 | tf_op jit(solution)/shard_map/ppermute | solution.py:19
  68.7 2.5 %collective-permute-done.2 = bf16[2,128,1024]{1,2,0:T(8,128)(2,1)S(1)} collective-permute-done((bf16[2,128,1024]{1,2,0:T(8,128)(2,1)S(1)}, bf16[2,128,1024]{1,2,0:T(8,128)(2,1)S(1)}, u32[]{:S(2)}, u32[]{:S(2)}) %collective-permute-start.2) | collective-permute-done | bytes 524320 | tf_op jit(solution)/shard_map/ppermute | solution.py:19
  73.3 8.9 %collective-permute-done.1 = bf16[2,128,1024]{1,2,0:T(8,128)(2,1)S(1)} collective-permute-done((bf16[2,128,1024]{1,2,0:T(8,128)(2,1)S(1)}, bf16[2,128,1024]{1,2,0:T(8,128)(2,1)S(1)}, u32[]{:S(2)}, u32[]{:S(2)}) %collective-permute-start.1) | collective-permute-done | bytes 524320 | tf_op jit(solution)/shard_map/ppermute | solution.py:19
  84.3 3.5 %collective-permute-done = bf16[2,128,1024]{1,2,0:T(8,128)(2,1)} collective-permute-done((bf16[2,128,1024]{1,2,0:T(8,128)(2,1)S(1)}, bf16[2,128,1024]{1,2,0:T(8,128)(2,1)}, u32[]{:S(2)}, u32[]{:S(2)}) %collective-permute-start) | collective-permute-done | bytes 524320 | tf_op jit(solution)/shard_map/ppermute | solution.py:19
  90.3 2.0 slice_bitcast_fusion.1
  94.1 2.4 %multiply_reduce_fusion = (f32[128]{0:T(128)S(1)}, f32[8,128,128]{2,1,0:T(8,128)}) fusion(f32[8,8,128,128]{3,2,1,0:T(8,128)S(1)} %get-tuple-element.336, f32[8,128]{1,0:T(8,128)S(1)} %log_add_fusion, pred[128,8,128]{0,2,1:T(8,128)(4,1)S(1)} %and_bitcast_fusion, bf16[2,8,128,8,128]{4,2,1,3,0:T(8,128)(2,1)S(1)} %maximum_dynamic-update-slice_fusion), kind=kOutput, calls=%fused_computation.76 | convolution fusion | flops 273153920 | bytes 6951424 | tf_op jit(solution)/shard_map/bhqsk,bskhd->bqhd/dot_general | solution.py:125
  97.9 10.9 %all-reduce = (f32[128]{0:T(128)S(1)}, f32[128]{0:T(128)S(1)}) all-reduce(f32[128]{0:T(128)S(1)} %get-tuple-element.337, f32[128]{0:T(128)S(1)} %fusion.45), channel_id=1, replica_groups=mesh['ctx'=64,'head'=4] {'head'}, use_global_device_ids=true, to_apply=%region_3.4 | all-reduce | flops 256 | bytes 2048 | tf_op jit(solution)/shard_map/psum | solution.py:129
  110.2 3.3 %fusion.3 = (bf16[8,8,128,128]{3,2,1,0:T(8,128)(2,1)S(1)}, f32[8,8,128,128]{2,3,1,0:T(8,128)S(1)}) fusion(f32[8,128]{1,0:T(8,128)S(1)} %log_add_fusion, pred[8,128,128]{2,1,0:T(8,128)(4,1)S(1)} %copy-done.13, bf16[128,8,128]{2,0,1:T(8,128)(2,1)} %copy_bitcast_fusion.1, bf16[8,128,8,128]{3,1,0,2:T(8,128)(2,1)} %get-tuple-element.327), kind=kOutput, calls=%fused_computation.8 | convolution fusion | flops 272629760 | bytes 8785920 | tf_op jit(solution)/shard_map/pqhd,pkhd->phqk/dot_general | solution.py:44
  113.5 2.2 multiply_convert_fusion
  118.6 2.2 collective-permute-start.6
  121.6 1.9 collective-permute-start.7
  124.4 1.9 collective-permute-start.8
  138.7 11.2 %collective-permute-done.7 = bf16[2,1,128,8,128]{2,4,3,1,0:T(8,128)(2,1)S(1)} collective-permute-done((bf16[2,1,128,8,128]{2,4,3,1,0:T(8,128)(2,1)}, bf16[2,1,128,8,128]{2,4,3,1,0:T(8,128)(2,1)S(1)}, u32[]{:S(2)}, u32[]{:S(2)}) %collective-permute-start.7) | collective-permute-done | bytes 524320 | tf_op jit(solution)/shard_map/ppermute | solution.py:19
  149.9 11.2 %collective-permute-done.8 = bf16[2,1,128,8,128]{2,4,3,1,0:T(8,128)(2,1)S(1)} collective-permute-done((bf16[2,1,128,8,128]{2,4,3,1,0:T(8,128)(2,1)}, bf16[2,1,128,8,128]{2,4,3,1,0:T(8,128)(2,1)S(1)}, u32[]{:S(2)}, u32[]{:S(2)}) %collective-permute-start.8) | collective-permute-done | bytes 524320 | tf_op jit(solution)/shard_map/ppermute | solution.py:19
  161.1 23.4 %collective-permute-done.9 = bf16[2,1,128,8,128]{2,4,3,1,0:T(8,128)(2,1)S(1)} collective-permute-done((bf16[2,1,128,8,128]{2,4,3,1,0:T(8,128)(2,1)}, bf16[2,1,128,8,128]{2,4,3,1,0:T(8,128)(2,1)S(1)}, u32[]{:S(2)}, u32[]{:S(2)}) %collective-permute-start.9) | collective-permute-done | bytes 524320 | tf_op jit(solution)/shard_map/ppermute | solution.py:19
  184.6 40.6 %collective-permute-done.10 = bf16[2,1,128,8,128]{2,4,3,1,0:T(8,128)(2,1)S(1)} collective-permute-done((bf16[2,1,128,8,128]{2,4,3,1,0:T(8,128)(2,1)}, bf16[2,1,128,8,128]{2,4,3,1,0:T(8,128)(2,1)S(1)}, u32[]{:S(2)}, u32[]{:S(2)}) %collective-permute-start.10) | collective-permute-done | bytes 524320 | tf_op jit(solution)/shard_map/ppermute | solution.py:19
  (101 shorter events, 46.6 us)
Async XLA Ops:
  0.6 41.8 %copy-start = (bf16[128,1024]{1,0:T(8,128)(2,1)S(1)}, bf16[128,1024]{1,0:T(8,128)(2,1)}, u32[]{:S(2)}) copy-start(bf16[128,1024]{1,0:T(8,128)(2,1)} %param.12) | copy-start | bytes 786436
  3.0 31.7 %collective-permute-start.5 = (bf16[2,128,1024]{1,2,0:T(8,128)(2,1)S(1)}, bf16[2,128,1024]{1,2,0:T(8,128)(2,1)}, u32[]{:S(2)}, u32[]{:S(2)}) collective-permute-start(bf16[2,128,1024]{1,2,0:T(8,128)(2,1)S(1)} %pad_maximum_fusion), channel_id=1, source_target_pairs={{0,128},{4,132},{8,136},{12,140},{16,144},{20,148},{24,152},{28,15... | collective-permute-start | bytes 1572872 | tf_op jit(solution)/shard_map/ppermute | solution.py:19
  11.1 45.2 %collective-permute-start.4 = (bf16[2,128,1024]{1,2,0:T(8,128)(2,1)S(1)}, bf16[2,128,1024]{1,2,0:T(8,128)(2,1)S(1)}, u32[]{:S(2)}, u32[]{:S(2)}) collective-permute-start(bf16[2,128,1024]{1,2,0:T(8,128)(2,1)S(1)} %pad_maximum_fusion), channel_id=1, source_target_pairs={{0,64},{4,68},{8,72},{12,76},{16,80},{20,84},{24,88},{28,92},{32,9... | collective-permute-start | bytes 1572872 | tf_op jit(solution)/shard_map/ppermute | solution.py:19
  13.0 53.6 %collective-permute-start.3 = (bf16[2,128,1024]{1,2,0:T(8,128)(2,1)S(1)}, bf16[2,128,1024]{1,2,0:T(8,128)(2,1)S(1)}, u32[]{:S(2)}, u32[]{:S(2)}) collective-permute-start(bf16[2,128,1024]{1,2,0:T(8,128)(2,1)S(1)} %pad_maximum_fusion), channel_id=1, source_target_pairs={{0,32},{4,36},{8,40},{12,44},{16,48},{20,52},{24,56},{28,60},{32,6... | collective-permute-start | bytes 1572872 | tf_op jit(solution)/shard_map/ppermute | solution.py:19
  15.9 55.2 %collective-permute-start.2 = (bf16[2,128,1024]{1,2,0:T(8,128)(2,1)S(1)}, bf16[2,128,1024]{1,2,0:T(8,128)(2,1)S(1)}, u32[]{:S(2)}, u32[]{:S(2)}) collective-permute-start(bf16[2,128,1024]{1,2,0:T(8,128)(2,1)S(1)} %pad_maximum_fusion), channel_id=1, source_target_pairs={{0,16},{4,20},{8,24},{12,28},{16,32},{20,36},{24,40},{28,44},{32,4... | collective-permute-start | bytes 1572872 | tf_op jit(solution)/shard_map/ppermute | solution.py:19
  20.9 61.3 %collective-permute-start.1 = (bf16[2,128,1024]{1,2,0:T(8,128)(2,1)S(1)}, bf16[2,128,1024]{1,2,0:T(8,128)(2,1)S(1)}, u32[]{:S(2)}, u32[]{:S(2)}) collective-permute-start(bf16[2,128,1024]{1,2,0:T(8,128)(2,1)S(1)} %pad_maximum_fusion), channel_id=1, source_target_pairs={{0,8},{4,12},{8,16},{12,20},{16,24},{20,28},{24,32},{28,36},{32,40... | collective-permute-start | bytes 1572872 | tf_op jit(solution)/shard_map/ppermute | solution.py:19
  24.3 12.3 %copy-start.14 = (pred[8]{0:T(512)(128)(4,1)}, pred[8]{0:T(512)(128)(4,1)S(1)}, u32[]{:S(2)}) copy-start(pred[8]{0:T(512)(128)(4,1)S(1)} %fusion.48) | copy-start | bytes 28
  24.3 12.3 %copy-start.15 = (pred[8]{0:T(512)(128)(4,1)}, pred[8]{0:T(512)(128)(4,1)S(1)}, u32[]{:S(2)}) copy-start(pred[8]{0:T(512)(128)(4,1)S(1)} %compare_not_fusion) | copy-start | bytes 28
  34.7 53.2 %collective-permute-start = (bf16[2,128,1024]{1,2,0:T(8,128)(2,1)S(1)}, bf16[2,128,1024]{1,2,0:T(8,128)(2,1)}, u32[]{:S(2)}, u32[]{:S(2)}) collective-permute-start(bf16[2,128,1024]{1,2,0:T(8,128)(2,1)S(1)} %pad_maximum_fusion), channel_id=1, source_target_pairs={{0,4},{4,8},{8,12},{12,16},{16,20},{20,24},{24,28},{28,32},{32,36}... | collective-permute-start | bytes 1572872 | tf_op jit(solution)/shard_map/ppermute | solution.py:19
  89.2 1.0 copy-start.6
  89.2 1.0 copy-start.7
  90.3 3.8 %copy-start.1 = (bf16[2,8,128,8,128]{4,2,1,3,0:T(8,128)(2,1)}, bf16[2,8,128,8,128]{4,2,1,3,0:T(8,128)(2,1)S(1)}, u32[]{:S(2)}) copy-start(bf16[2,8,128,8,128]{4,2,1,3,0:T(8,128)(2,1)S(1)} %maximum_dynamic-update-slice_fusion) | copy-start | bytes 12582916
  90.3 2.0 copy-start.12
  94.1 3.7 %copy-start.5 = (bf16[128,1024]{1,0:T(8,128)(2,1)S(1)}, bf16[128,1024]{1,0:T(8,128)(2,1)}, u32[]{:S(2)}) copy-start(bf16[128,1024]{1,0:T(8,128)(2,1)} %param.16) | copy-start | bytes 786436
  96.4 13.7 %copy-start.13 = (pred[8,128,128]{2,1,0:T(8,128)(4,1)S(1)}, pred[8,128,128]{2,1,0:T(8,128)(4,1)}, u32[]{:S(2)}) copy-start(pred[8,128,128]{2,1,0:T(8,128)(4,1)} %or_and_fusion) | copy-start | bytes 393220
  113.4 18.7 %copy-start.3 = (bf16[8,8,128,128]{3,2,1,0:T(8,128)(2,1)}, bf16[8,8,128,128]{3,2,1,0:T(8,128)(2,1)S(1)}, u32[]{:S(2)}) copy-start(bf16[8,8,128,128]{3,2,1,0:T(8,128)(2,1)S(1)} %get-tuple-element.339) | copy-start | bytes 6291460
  115.6 18.9 %copy-start.4 = (bf16[8,8,128,128]{3,2,1,0:T(8,128)(2,1)}, bf16[8,8,128,128]{3,2,1,0:T(8,128)(2,1)S(1)}, u32[]{:S(2)}) copy-start(bf16[8,8,128,128]{3,2,1,0:T(8,128)(2,1)S(1)} %multiply_convert_fusion) | copy-start | bytes 6291460
  118.2 16.4 %copy-start.2 = (bf16[2,8,128,8,128]{4,2,1,3,0:T(8,128)(2,1)S(1)}, bf16[2,8,128,8,128]{4,2,1,3,0:T(8,128)(2,1)}, u32[]{:S(2)}) copy-start(bf16[2,8,128,8,128]{4,2,1,3,0:T(8,128)(2,1)} %copy-done.1) | copy-start | bytes 12582916
  118.6 14.7 %collective-permute-start.6 = (bf16[2,1,128,8,128]{2,4,3,1,0:T(8,128)(2,1)S(1)}, bf16[2,1,128,8,128]{2,4,3,1,0:T(8,128)(2,1)S(1)}, u32[]{:S(2)}, u32[]{:S(2)}) collective-permute-start(bf16[2,1,128,8,128]{2,4,3,1,0:T(8,128)(2,1)S(1)} %pad_maximum_fusion.1), channel_id=1, source_target_pairs={{4,0},{8,4},{12,8},{16,12},{20,16},{24,20},{28,24},{32,28},{36,32}... | collective-permute-start | bytes 1572872 | tf_op jit(solution)/shard_map/ppermute | solution.py:19
  121.6 28.3 %collective-permute-start.7 = (bf16[2,1,128,8,128]{2,4,3,1,0:T(8,128)(2,1)}, bf16[2,1,128,8,128]{2,4,3,1,0:T(8,128)(2,1)S(1)}, u32[]{:S(2)}, u32[]{:S(2)}) collective-permute-start(bf16[2,1,128,8,128]{2,4,3,1,0:T(8,128)(2,1)} %pad_maximum_fusion.2), channel_id=1, source_target_pairs={{8,0},{12,4},{16,8},{20,12},{24,16},{28,20},{32,24},{36,28},{40,32... | collective-permute-start | bytes 1572872 | tf_op jit(solution)/shard_map/ppermute | solution.py:19
  124.4 36.8 %collective-permute-start.8 = (bf16[2,1,128,8,128]{2,4,3,1,0:T(8,128)(2,1)}, bf16[2,1,128,8,128]{2,4,3,1,0:T(8,128)(2,1)S(1)}, u32[]{:S(2)}, u32[]{:S(2)}) collective-permute-start(bf16[2,1,128,8,128]{2,4,3,1,0:T(8,128)(2,1)} %pad_maximum_fusion.3), channel_id=1, source_target_pairs={{16,0},{20,4},{24,8},{28,12},{32,16},{36,20},{40,24},{44,28},{48,3... | collective-permute-start | bytes 1572872 | tf_op jit(solution)/shard_map/ppermute | solution.py:19
  127.1 57.4 %collective-permute-start.9 = (bf16[2,1,128,8,128]{2,4,3,1,0:T(8,128)(2,1)}, bf16[2,1,128,8,128]{2,4,3,1,0:T(8,128)(2,1)S(1)}, u32[]{:S(2)}, u32[]{:S(2)}) collective-permute-start(bf16[2,1,128,8,128]{2,4,3,1,0:T(8,128)(2,1)} %pad_maximum_fusion.4), channel_id=1, source_target_pairs={{32,0},{36,4},{40,8},{44,12},{48,16},{52,20},{56,24},{60,28},{64,3... | collective-permute-start | bytes 1572872 | tf_op jit(solution)/shard_map/ppermute | solution.py:19
  129.9 95.2 %collective-permute-start.10 = (bf16[2,1,128,8,128]{2,4,3,1,0:T(8,128)(2,1)}, bf16[2,1,128,8,128]{2,4,3,1,0:T(8,128)(2,1)S(1)}, u32[]{:S(2)}, u32[]{:S(2)}) collective-permute-start(bf16[2,1,128,8,128]{2,4,3,1,0:T(8,128)(2,1)} %pad_maximum_fusion.5), channel_id=1, source_target_pairs={{64,0},{68,4},{72,8},{76,12},{80,16},{84,20},{88,24},{92,28},{96,3... | collective-permute-start | bytes 1572872 | tf_op jit(solution)/shard_map/ppermute | solution.py:19
  133.3 91.8 %collective-permute-start.11 = (bf16[2,1,128,8,128]{2,4,3,1,0:T(8,128)(2,1)}, bf16[2,1,128,8,128]{2,4,3,1,0:T(8,128)(2,1)}, u32[]{:S(2)}, u32[]{:S(2)}) collective-permute-start(bf16[2,1,128,8,128]{2,4,3,1,0:T(8,128)(2,1)} %pad_maximum_fusion.6), channel_id=1, source_target_pairs={{128,0},{132,4},{136,8},{140,12},{144,16},{148,20},{152,24},{156,2... | collective-permute-start | bytes 1572872 | tf_op jit(solution)/shard_map/ppermute | solution.py:19
  (4 other events, 3.2 us)
where the time goes:
time: 230 us; the launch traced here: 228 us
  waiting for transfers between devices  132 us (57%)
  starting transfers between devices  33.4 us (15%)
  local copies, waits for them, and re-layouts  25.3 us (11%)
  matrix products  15.2 us (7%)
  blocking collectives  10.9 us (5%)
  other arithmetic  10.8 us (5%)
    ppermute x12, waiting for transfers between devices, shifted(): return lax.ppermute(block, axis, route)  132 us
    ppermute x12, starting transfers between devices, shifted(): return lax.ppermute(block, axis, route)  33.4 us
    psum x1, blocking collectives, shards(): square_sum = lax.psum(jnp.sum(attn_wide * attn_wide, axis=1), 'head')  10.9 us
    unnamed x46, local copies, waits for them, and re-layouts  10.8 us
    another operation x6, local copies, waits for them, and re-layouts, shards(): pair_kv = jnp.stack(gathered, axis=1)  7.87 us
  transfers between devices with their start and end apart: 12, of which 10 were waited for; matrix products, arithmetic and copies ran while one was open for 10% of the time, Pallas kernels for 0%

commit v1 on v0

v1 whole, which is shorter than its diff:
```python
import functools
import math

import jax
import jax.numpy as jnp
from jax import lax
from jax.experimental import pallas as pl
from jax.experimental.pallas import tpu as pltpu
from jax.sharding import PartitionSpec as P

HD = 128
BLOCK = 128
WIDTH = 4096
HEADS = 8
SLOTS = 7
OWN = 6
BLOCKS = 64
CHUNKS = 4
PER = HEADS // CHUNKS
NEG_BIG = -1e30
EPSILON = 1e-06
SCALE = HD**-0.5
SCALE2 = SCALE * math.log2(math.e)
MESH = pl.DeviceIdType.MESH
F32 = jnp.float32
BF16 = jnp.bfloat16


def nt(a, b):
    return lax.dot_general(a, b, (((1,), (1,)), ((), ())), preferred_element_type=F32)


def nn(a, b):
    return lax.dot_general(a, b, (((1,), (0,)), ((), ())), preferred_element_type=F32)


class Flow:
    def __init__(self, buf, send_sem, recv_sem, place, head, mirrored):
        self.buf, self.send_sem, self.recv_sem = buf, send_sem, recv_sem
        self.mirrored, self.head = mirrored, head
        self.j = BLOCKS - 1 - place if mirrored else place
        self.z, self.x, self.c = self.j // 8, (self.j // 2) % 4, self.j % 2

    def to(self, z, x, c):
        index = z * 8 + x * 2 + c
        index = BLOCKS - 1 - index if self.mirrored else index
        return (lax.rem(index + BLOCKS, BLOCKS), self.head)

    def copy(self, g, source, k, target=None):
        rows = pl.ds(g * PER, PER)
        return pltpu.make_async_remote_copy(
            src_ref=self.buf.at[rows, source],
            dst_ref=self.buf.at[rows, k],
            send_sem=self.send_sem.at[g, k],
            recv_sem=self.recv_sem.at[g, k],
            device_id=target or self.to(self.z, self.x, 1 - self.c),
            device_id_type=MESH,
        )

    def send(self, condition, g, source, k, z, x, c):
        @pl.when(condition)
        def _():
            self.copy(g, source, k, self.to(z, x, c)).start()

    def own(self, g):
        z, x, c = self.z, self.x, self.c
        self.send(z < 7, g, OWN, 3, z + 1, x, c)
        self.send((z == 1) | (z == 3), g, OWN, 5, z + 4, x, c)
        self.send(x < 3, g, OWN, 1, z, x + 1, c)
        self.send(x < 2, g, OWN, 2, z, x + 2, c)
        self.send(c == 0, g, OWN, 0, z, x, 1)

    def stage_a(self, g):
        z, x, c = self.z, self.x, self.c

        @pl.when(z >= 1)
        def _():
            self.copy(g, OWN, 3).wait_recv()
            self.send(z < 7, g, 3, 4, z + 1, x, c)
            self.send(x == 3, g, 3, 1, z, 0, c)
            self.send(x >= 2, g, 3, 2, z, x - 2, c)

    def stage_b(self, g):
        z, x, c = self.z, self.x, self.c

        @pl.when(z >= 2)
        def _():
            self.copy(g, OWN, 4).wait_recv()
            self.send((z == 2) | (z == 4), g, 4, 5, z + 2, x, c)

        @pl.when(self.j >= 2)
        def _():
            self.copy(g, OWN, 1).wait_recv()
            self.send(c == 1, g, 1, 0, z, x, 0)

    def stage_c(self, g):
        for condition, k in ((self.j >= 1, 0), (self.j >= 4, 2), (self.z >= 4, 5)):

            @pl.when(condition)
            def _():
                self.copy(g, OWN, k).wait_recv()

    def drain(self, g):
        z, x, c, j = self.z, self.x, self.c, self.j
        for condition, k in (
            ((c == 0) | (j >= 2), 0),
            ((x < 3) | (z >= 1), 1),
            ((x < 2) | (z >= 1), 2),
            (z < 7, 3),
            ((z >= 1) & (z < 7), 4),
            ((z >= 1) & (z <= 4), 5),
        ):

            @pl.when(condition)
            def _():
                self.copy(g, OWN, k).wait_send()

    def clear(self):
        for k in range(6):

            @pl.when(self.j < 2**k)
            def _():
                self.buf[:, k] = jnp.zeros(self.buf.shape[:1] + self.buf.shape[2:], self.buf.dtype)


def kernel(
    q_ref,
    k_ref,
    v_ref,
    pattern_ref,
    u_ref,
    normed_ref,
    dq_ref,
    dk_ref,
    dv_ref,
    kv,
    qs,
    gs,
    up,
    attn,
    probs,
    probs_t,
    row_scale,
    delta,
    stat_tile,
    stats,
    squares,
    crosses,
    y_buf,
    load_sem,
    kv_send,
    kv_recv,
    q_send,
    q_recv,
    g_send,
    g_recv,
    stat_send,
    stat_recv,
    y_send,
    y_recv,
):
    place = lax.axis_index("ctx")
    head = lax.axis_index("head")
    heads = lax.axis_size("head")
    z, x, c = place // 8, (place // 2) % 4, place % 2

    loads = []
    for h in range(HEADS):
        columns = pl.ds(h * HD, HD)
        for a, (ref, target) in enumerate(
            (
                (k_ref, kv.at[h, OWN, 0]),
                (v_ref, kv.at[h, OWN, 1]),
                (q_ref, qs.at[h, OWN]),
                (u_ref, up.at[h]),
            )
        ):
            copy = pltpu.make_async_copy(ref.at[:, columns], target, load_sem.at[a, h])
            copy.start()
            loads.append(copy)

    barrier = pltpu.get_barrier_semaphore()

    def ring(dz, dx, dc):
        return ((z + dz) % 8) * 8 + ((x + dx) % 4) * 2 + (c + dc) % 2

    partners = [(ring(d, 0, 0), head) for d in (1, 2, 4, 6, 7)]
    partners += [(ring(0, d, 0), head) for d in (1, 2, 3)]
    partners += [(ring(0, 0, 1), head)]
    partners += [((place + d) % BLOCKS, head) for d in (1, 2, 4, 60, 62, 63)]
    partners += [(place, (head + d) % heads) for d in range(1, heads)]
    for partner in partners:
        pl.semaphore_signal(barrier, inc=1, device_id=partner, device_id_type=MESH)

    kv_flow = Flow(kv, kv_send, kv_recv, place, head, False)
    q_flow = Flow(qs, q_send, q_recv, place, head, True)
    g_flow = Flow(gs, g_send, g_recv, place, head, True)
    for flow in (kv_flow, q_flow, g_flow):
        flow.clear()
    for k in range(6):

        @pl.when(g_flow.j < 2**k)
        def _():
            stats[k] = jnp.zeros(stats.shape[1:], F32)

    squares[...] = jnp.zeros(squares.shape, F32)
    crosses[...] = jnp.zeros(crosses.shape, F32)
    stat_tile[...] = jnp.zeros(stat_tile.shape, F32)
    for copy in loads:
        copy.wait()
    pl.semaphore_wait(barrier, len(partners))

    def every(body, count=CHUNKS):
        def step(g, carry):
            body(g)
            return carry

        lax.fori_loop(0, count, step, 0)

    every(kv_flow.own)
    every(q_flow.own)

    row = lax.broadcasted_iota(jnp.int32, (BLOCK, BLOCK), 0)
    lane = lax.broadcasted_iota(jnp.int32, (BLOCK, BLOCK), 1)

    def bias_of(index, k):
        return jnp.where(pattern_ref[index, k] >= 0, 0.0, NEG_BIG).astype(F32)

    def slot(array, s):
        return array[:, s * BLOCK : (s + 1) * BLOCK]

    def put(ref, h, value):
        ref[:, pl.ds(pl.multiple_of(h * HD, HD), HD)] = value

    def forward(h):
        raw = nt(qs[h, OWN], kv[h, :, 0].reshape(SLOTS * BLOCK, HD))
        scores = [slot(raw, s) * SCALE2 + bias_of(place, s) for s in range(OWN)]
        scores.append(jnp.where(lane <= row, slot(raw, OWN) * SCALE2, NEG_BIG))
        highest = jnp.max(functools.reduce(jnp.maximum, scores), axis=1, keepdims=True)
        weights = [jnp.exp2(s - highest) for s in scores]
        total = jnp.sum(functools.reduce(jnp.add, weights), axis=1, keepdims=True)
        inverse_total = 1.0 / total
        rounded = jnp.concatenate([w.astype(BF16) for w in weights], axis=1)
        probs[h] = rounded
        out = nn(rounded, kv[h, :, 1].reshape(SLOTS * BLOCK, HD)) * inverse_total
        out = out.astype(BF16)
        attn[h] = out
        wide = out.astype(F32)
        squares[...] += wide * wide
        crosses[...] += wide * up[h].astype(F32)
        row_scale[h] = inverse_total * SCALE
        stat_tile[...] = jnp.where(lane == h, highest + jnp.log2(total), stat_tile[...])

    def heads_of(g, body):
        def step(i, carry):
            body(g * PER + i)
            return carry

        lax.fori_loop(0, PER, step, 0)

    def first_phase(s):
        @pl.when(s < CHUNKS)
        def _():
            kv_flow.stage_a(s)

        @pl.when((s >= 1) & (s <= CHUNKS))
        def _():
            kv_flow.stage_b(s - 1)
            q_flow.stage_a(s - 1)

        @pl.when(s >= 2)
        def _():
            q_flow.stage_b(s - 2)
            kv_flow.stage_c(s - 2)
            heads_of(s - 2, forward)

    every(first_phase, CHUNKS + 2)

    square = jnp.sum(squares[...], axis=1, keepdims=True)
    cross = jnp.sum(crosses[...], axis=1, keepdims=True)
    tile = jnp.where(lane == 0, square, jnp.where(lane == 1, cross, 0.0))
    y_buf[heads - 1] = tile.T[:8]
    copies = []
    for d in range(1, heads):
        copy = pltpu.make_async_remote_copy(
            src_ref=y_buf.at[heads - 1],
            dst_ref=y_buf.at[d - 1],
            send_sem=y_send.at[d - 1],
            recv_sem=y_recv.at[d - 1],
            device_id=(place, (head + d) % heads),
            device_id_type=MESH,
        )
        copy.start()
        copies.append(copy)
    for copy in copies:
        copy.wait_recv()
    sums = functools.reduce(jnp.add, [y_buf[d] for d in range(heads)])
    sums = jnp.concatenate([sums, jnp.zeros((BLOCK - 8, BLOCK), F32)], axis=0).T
    inverse = lax.rsqrt(sums[:, 0:1] / WIDTH + EPSILON)
    factor = inverse * inverse * inverse * sums[:, 1:2] / WIDTH

    def gradient(h):
        wide = attn[h].astype(F32)
        grad = (inverse * up[h].astype(F32) - wide * factor).astype(BF16)
        gs[h, OWN] = grad
        put(normed_ref, h, (wide * inverse).astype(BF16))
        here = jnp.sum(grad.astype(F32) * wide, axis=1, keepdims=True)
        delta[h] = here
        stat_tile[...] = jnp.where(lane == h + HEADS, here, stat_tile[...])

    def gradient_chunk(g):
        heads_of(g, gradient)
        g_flow.own(g)

    every(gradient_chunk)

    stats[OWN] = stat_tile[...].T[: 2 * HEADS]

    def stat_copy(k):
        return pltpu.make_async_remote_copy(
            src_ref=stats.at[OWN],
            dst_ref=stats.at[k],
            send_sem=stat_send.at[k],
            recv_sem=stat_recv.at[k],
            device_id=(lax.rem(place - 2**k + BLOCKS, BLOCKS), head),
            device_id_type=MESH,
        )

    for k in range(6):

        @pl.when(place >= 2**k)
        def _():
            stat_copy(k).start()

    def grad_query(h):
        grad_probs = nt(gs[h, OWN], kv[h, :, 1].reshape(SLOTS * BLOCK, HD))
        held = probs[h].astype(F32)
        dscore = (held * (grad_probs - delta[h]) * row_scale[h]).astype(BF16)
        put(dq_ref, h, nn(dscore, kv[h, :, 0].reshape(SLOTS * BLOCK, HD)).astype(BF16))

    def key_probs(h):
        raw = nt(kv[h, OWN, 0], qs[h].reshape(SLOTS * BLOCK, HD))
        parts = []
        for s in range(SLOTS):
            scores = slot(raw, s) * SCALE2 - stats[s, pl.ds(h, 1), :]
            if s == OWN:
                scores = jnp.where(row <= lane, scores, NEG_BIG)
            else:
                index = place + 2**s
                live = (pattern_ref[jnp.minimum(index, BLOCKS - 1), s] >= 0) & (index < BLOCKS)
                scores = scores + jnp.where(live, 0.0, NEG_BIG).astype(F32)
            parts.append(jnp.exp2(scores).astype(BF16))
        probs_t[h] = jnp.concatenate(parts, axis=1)

    def grad_keys(h):
        grads = gs[h].reshape(SLOTS * BLOCK, HD)
        held = probs_t[h]
        put(dv_ref, h, nn(held, grads).astype(BF16))
        raw = nt(kv[h, OWN, 1], grads)
        parts = []
        for s in range(SLOTS):
            part = slot(raw, s) - stats[s, pl.ds(h + HEADS, 1), :]
            parts.append((slot(held, s).astype(F32) * part * SCALE).astype(BF16))
        dscore = jnp.concatenate(parts, axis=1)
        put(dk_ref, h, nn(dscore, qs[h].reshape(SLOTS * BLOCK, HD)).astype(BF16))

    def second_phase(s):
        @pl.when(s < CHUNKS)
        def _():
            heads_of(s, grad_query)
            g_flow.stage_a(s)

        @pl.when(s == 1)
        def _():
            for k in range(6):

                @pl.when(place + 2**k < BLOCKS)
                def _():
                    stat_copy(k).wait_recv()

        @pl.when((s >= 1) & (s <= CHUNKS))
        def _():
            g_flow.stage_b(s - 1)
            q_flow.stage_c(s - 1)
            heads_of(s - 1, key_probs)

        @pl.when(s >= 2)
        def _():
            g_flow.stage_c(s - 2)
            heads_of(s - 2, grad_keys)

    every(second_phase, CHUNKS + 2)

    every(kv_flow.drain)
    every(q_flow.drain)
    every(g_flow.drain)
    for copy in copies:
        copy.wait_send()
    for k in range(6):

        @pl.when(place >= 2**k)
        def _():
            stat_copy(k).wait_send()


def shards(queries, keys, values, pattern, upstream):
    heads = lax.axis_size("head")
    tokens, width = queries.shape
    out = jax.ShapeDtypeStruct((tokens, width), BF16)
    tile = (BLOCK, HD)
    dma = pltpu.SemaphoreType.DMA
    anywhere = pl.BlockSpec(memory_space=pl.ANY)
    return pl.pallas_call(
        kernel,
        out_shape=(out,) * 4,
        in_specs=[
            anywhere,
            anywhere,
            anywhere,
            pl.BlockSpec(memory_space=pltpu.SMEM),
            anywhere,
        ],
        out_specs=[pl.BlockSpec(memory_space=pltpu.VMEM)] * 4,
        scratch_shapes=[
            pltpu.VMEM((HEADS, SLOTS, 2) + tile, BF16),
            pltpu.VMEM((HEADS, SLOTS) + tile, BF16),
            pltpu.VMEM((HEADS, SLOTS) + tile, BF16),
            pltpu.VMEM((HEADS,) + tile, BF16),
            pltpu.VMEM((HEADS,) + tile, BF16),
            pltpu.VMEM((HEADS, BLOCK, SLOTS * BLOCK), BF16),
            pltpu.VMEM((HEADS, BLOCK, SLOTS * BLOCK), BF16),
            pltpu.VMEM((HEADS, BLOCK, 1), F32),
            pltpu.VMEM((HEADS, BLOCK, 1), F32),
            pltpu.VMEM((BLOCK, BLOCK), F32),
            pltpu.VMEM((SLOTS, 2 * HEADS, BLOCK), F32),
            pltpu.VMEM(tile, F32),
            pltpu.VMEM(tile, F32),
            pltpu.VMEM((heads, 8, BLOCK), F32),
            dma((4, HEADS)),
            dma((CHUNKS, 6)),
            dma((CHUNKS, 6)),
            dma((CHUNKS, 6)),
            dma((CHUNKS, 6)),
            dma((CHUNKS, 6)),
            dma((CHUNKS, 6)),
            dma((6,)),
            dma((6,)),
            dma((heads - 1,)),
            dma((heads - 1,)),
        ],
        compiler_params=pltpu.CompilerParams(
            collective_id=0, has_side_effects=True, vmem_limit_bytes=48 * 1024 * 1024
        ),
        cost_estimate=pl.CostEstimate(
            flops=2_000_000_000, bytes_accessed=2 * 1024 * 1024, transcendentals=2_000_000
        ),
    )(queries, keys, values, pattern, upstream)


def solution(mesh):
    return jax.shard_map(
        shards,
        mesh=mesh,
        in_specs=(P("ctx", "head"), P("ctx", "head"), P("ctx", "head"), P(), P("ctx", "head")),
        out_specs=(P("ctx", "head"), P("ctx", "head"), P("ctx", "head"), P("ctx", "head")),
        check_vma=False,
    )
```

time: 230 us -> 91 us (0.40)
  the two profiles are of different devices: /device:TPU:64 before, /device:TPU:1 now
where the time goes in v1:
time: 91 us; the launch traced here: 90.2 us
  Pallas kernels  82.2 us (90%)
  local copies, waits for them, and re-layouts  7.38 us (8%)
    pallas_call x1, Pallas kernels, shards(): pl.pallas_call(kernel, out_shape=(out,) * 4, in_specs=[anywhere, anywhere...  82.2 us
    unnamed x13, local copies, waits for them, and re-layouts  7.38 us

profile of v1, /device:TPU:1, one launch (start us, length us, event | category | flops | bytes accessed | tf_op | source)
XLA Modules:
  0.0 90.2 jit_solution(17817944684868940942)
XLA Ops:
  0.6 0.8 copy.9.pattern_ref
  1.4 0.0 copy-start
  1.4 0.9 %copy-done = bf16[128,1024]{1,0:T(8,128)(2,1)S(1)} copy-done((bf16[128,1024]{1,0:T(8,128)(2,1)S(1)}, bf16[128,1024]{1,0:T(8,128)(2,1)}, u32[]{:S(2)}) %copy-start) | copy-done | bytes 262168
  2.4 0.0 copy-start.1
  2.4 0.9 %copy-done.1 = bf16[128,1024]{1,0:T(8,128)(2,1)S(1)} copy-done((bf16[128,1024]{1,0:T(8,128)(2,1)S(1)}, bf16[128,1024]{1,0:T(8,128)(2,1)}, u32[]{:S(2)}) %copy-start.1) | copy-done | bytes 262168
  3.3 0.0 copy-start.2
  3.3 0.9 %copy-done.2 = bf16[128,1024]{1,0:T(8,128)(2,1)S(1)} copy-done((bf16[128,1024]{1,0:T(8,128)(2,1)S(1)}, bf16[128,1024]{1,0:T(8,128)(2,1)}, u32[]{:S(2)}) %copy-start.2) | copy-done | bytes 262168
  4.3 0.0 copy-start.3
  4.3 0.9 %copy-done.3 = bf16[128,1024]{1,0:T(8,128)(2,1)S(1)} copy-done((bf16[128,1024]{1,0:T(8,128)(2,1)S(1)}, bf16[128,1024]{1,0:T(8,128)(2,1)}, u32[]{:S(2)}) %copy-start.3) | copy-done | bytes 262168
  5.2 82.2 %shard_map.84 = (bf16[128,1024]{1,0:T(8,128)(2,1)S(1)}, bf16[128,1024]{1,0:T(8,128)(2,1)S(1)}, bf16[128,1024]{1,0:T(8,128)(2,1)S(1)}, bf16[128,1024]{1,0:T(8,128)(2,1)S(1)}) custom-call(bf16[128,1024]{1,0:T(8,128)(2,1)S(1)} %copy-done, bf16[128,1024]{1,0:T(8,128)(2,1)S(1)} %copy-done.1, bf16[128,1024]{1,0:T(8,128)(2,1)S(1)} %copy-done.2, ...), custom_call_target="tpu_custom_call" | custom-call | flops 2000000000 | bytes 2097152 | tf_op jit(solution)/shard_map/pallas_call | solution.py:413
  87.4 0.7 copy.14
  88.1 0.7 copy.15
  88.8 0.7 copy.16
  89.5 0.7 copy.17
Async XLA Ops:
  1.4 0.9 %copy-start = (bf16[128,1024]{1,0:T(8,128)(2,1)S(1)}, bf16[128,1024]{1,0:T(8,128)(2,1)}, u32[]{:S(2)}) copy-start(bf16[128,1024]{1,0:T(8,128)(2,1)} %q_ref.1) | copy-start | bytes 786436
  2.4 0.9 %copy-start.1 = (bf16[128,1024]{1,0:T(8,128)(2,1)S(1)}, bf16[128,1024]{1,0:T(8,128)(2,1)}, u32[]{:S(2)}) copy-start(bf16[128,1024]{1,0:T(8,128)(2,1)} %k_ref.1) | copy-start | bytes 786436
  3.3 0.9 %copy-start.2 = (bf16[128,1024]{1,0:T(8,128)(2,1)S(1)}, bf16[128,1024]{1,0:T(8,128)(2,1)}, u32[]{:S(2)}) copy-start(bf16[128,1024]{1,0:T(8,128)(2,1)} %v_ref.1) | copy-start | bytes 786436
  4.3 0.9 %copy-start.3 = (bf16[128,1024]{1,0:T(8,128)(2,1)S(1)}, bf16[128,1024]{1,0:T(8,128)(2,1)}, u32[]{:S(2)}) copy-start(bf16[128,1024]{1,0:T(8,128)(2,1)} %u_ref.1) | copy-start | bytes 786436

commit v2 on v1

--- a/solution.py
+++ b/solution.py
@@ -14,9 +14,12 @@
 HEADS = 8
 SLOTS = 7
 OWN = 6
+LEVELS = 7
 BLOCKS = 64
 CHUNKS = 4
+VMEM = 63 * 1024 * 1024
 PER = HEADS // CHUNKS
+LEAD = 1
 NEG_BIG = -1e30
 EPSILON = 1e-06
 SCALE = HD**-0.5
@@ -65,10 +68,13 @@
     def own(self, g):
         z, x, c = self.z, self.x, self.c
         self.send(z < 7, g, OWN, 3, z + 1, x, c)
-        self.send((z == 1) | (z == 3), g, OWN, 5, z + 4, x, c)
         self.send(x < 3, g, OWN, 1, z, x + 1, c)
         self.send(x < 2, g, OWN, 2, z, x + 2, c)
         self.send(c == 0, g, OWN, 0, z, x, 1)
+
+    def far(self, g):
+        z, x, c = self.z, self.x, self.c
+        self.send((z == 1) | (z == 3), g, OWN, 5, z + 4, x, c)
 
     def stage_a(self, g):
         z, x, c = self.z, self.x, self.c
@@ -127,12 +133,14 @@
     q_ref,
     k_ref,
     v_ref,
-    pattern_ref,
+    pattern_hbm,
     u_ref,
     normed_ref,
     dq_ref,
     dk_ref,
     dv_ref,
+    pattern_ref,
+    staged,
     kv,
     qs,
     gs,
@@ -147,7 +155,9 @@
     squares,
     crosses,
     y_buf,
+    pattern_sem,
     load_sem,
+    store_sem,
     kv_send,
     kv_recv,
     q_send,
@@ -164,7 +174,20 @@
     heads = lax.axis_size("head")
     z, x, c = place // 8, (place // 2) % 4, place % 2
 
-    loads = []
+    barrier = pltpu.get_barrier_semaphore()
+
+    def ring(dz, dx, dc):
+        return ((z + dz) % 8) * 8 + ((x + dx) % 4) * 2 + (c + dc) % 2
+
+    partners = [(ring(d, 0, 0), head) for d in (1, 2, 4, 6, 7)]
+    partners += [(ring(0, d, 0), head) for d in (1, 2, 3)]
+    partners += [(ring(0, 0, 1), head)]
+    partners += [((place + d) % BLOCKS, head) for d in (1, 2, 4, 60, 62, 63)]
+    partners += [(place, (head + d) % heads) for d in range(1, heads)]
+    for partner in partners:
+        pl.semaphore_signal(barrier, inc=1, device_id=partner, device_id_type=MESH)
+
+    loads = [pltpu.make_async_copy(pattern_hbm, pattern_ref, pattern_sem)]
     for h in range(HEADS):
         columns = pl.ds(h * HD, HD)
         for a, (ref, target) in enumerate(
@@ -176,21 +199,9 @@
             )
         ):
             copy = pltpu.make_async_copy(ref.at[:, columns], target, load_sem.at[a, h])
-            copy.start()
             loads.append(copy)
-
-    barrier = pltpu.get_barrier_semaphore()
-
-    def ring(dz, dx, dc):
-        return ((z + dz) % 8) * 8 + ((x + dx) % 4) * 2 + (c + dc) % 2
-
-    partners = [(ring(d, 0, 0), head) for d in (1, 2, 4, 6, 7)]
-    partners += [(ring(0, d, 0), head) for d in (1, 2, 3)]
-    partners += [(ring(0, 0, 1), head)]
-    partners += [((place + d) % BLOCKS, head) for d in (1, 2, 4, 60, 62, 63)]
-    partners += [(place, (head + d) % heads) for d in range(1, heads)]
-    for partner in partners:
-        pl.semaphore_signal(barrier, inc=1, device_id=partner, device_id_type=MESH)
+    for copy in loads:
+        copy.start()
 
     kv_flow = Flow(kv, kv_send, kv_recv, place, head, False)
     q_flow = Flow(qs, q_send, q_recv, place, head, True)
@@ -217,20 +228,32 @@
 
         lax.fori_loop(0, count, step, 0)
 
-    every(kv_flow.own)
-    every(q_flow.own)
+    def kv_send_chunk(g):
+        kv_flow.own(g)
+        kv_flow.far(g)
+
+    every(kv_send_chunk, LEAD)
 
     row = lax.broadcasted_iota(jnp.int32, (BLOCK, BLOCK), 0)
     lane = lax.broadcasted_iota(jnp.int32, (BLOCK, BLOCK), 1)
 
     def bias_of(index, k):
-        return jnp.where(pattern_ref[index, k] >= 0, 0.0, NEG_BIG).astype(F32)
+        return jnp.where(pattern_ref[k, index] >= 0, 0.0, NEG_BIG).astype(F32)
 
     def slot(array, s):
         return array[:, s * BLOCK : (s + 1) * BLOCK]
 
-    def put(ref, h, value):
-        ref[:, pl.ds(pl.multiple_of(h * HD, HD), HD)] = value
+    results = (normed_ref, dq_ref, dk_ref, dv_ref)
+
+    def store(a, h):
+        columns = pl.ds(pl.multiple_of(h * HD, HD), HD)
+        return pltpu.make_async_copy(
+            staged.at[a, h], results[a].at[:, columns], store_sem.at[a, h]
+        )
+
+    def put(a, h, value):
+        staged[a, h] = value
+        store(a, h).start()
 
     def forward(h):
         raw = nt(qs[h, OWN], kv[h, :, 0].reshape(SLOTS * BLOCK, HD))
@@ -263,18 +286,51 @@
         def _():
             kv_flow.stage_a(s)
 
+        @pl.when(s < CHUNKS - LEAD)
+        def _():
+            kv_send_chunk(s + LEAD)
+
         @pl.when((s >= 1) & (s <= CHUNKS))
         def _():
             kv_flow.stage_b(s - 1)
-            q_flow.stage_a(s - 1)
+
+        @pl.when(s < CHUNKS)
+        def _():
+            q_flow.own(s)
 
         @pl.when(s >= 2)
         def _():
-            q_flow.stage_b(s - 2)
+            q_flow.stage_a(s - 2)
             kv_flow.stage_c(s - 2)
             heads_of(s - 2, forward)
 
     every(first_phase, CHUNKS + 2)
+
+    stats[OWN, 0] = stat_tile[...].T[:HEADS]
+
+    def stat_copy(k, part):
+        return pltpu.make_async_remote_copy(
+            src_ref=stats.at[OWN, part],
+            dst_ref=stats.at[k, part],
+            send_sem=stat_send.at[k, part],
+            recv_sem=stat_recv.at[k, part],
+            device_id=(lax.rem(place - 2**k + BLOCKS, BLOCKS), head),
+            device_id_type=MESH,
+        )
+
+    def stat_start(part):
+        for k in range(6):
+
+            @pl.when(place >= 2**k)
+            def _():
+                stat_copy(k, part).start()
+
+    def stat_wait(part):
+        for k in range(6):
+
+            @pl.when(place + 2**k < BLOCKS)
+            def _():
+                stat_copy(k, part).wait_recv()
 
     square = jnp.sum(squares[...], axis=1, keepdims=True)
     cross = jnp.sum(crosses[...], axis=1, keepdims=True)
@@ -292,6 +348,13 @@
         )
         copy.start()
         copies.append(copy)
+    stat_start(0)
+
+    def q_rest(g):
+        q_flow.far(g)
+        q_flow.stage_b(g)
+
+    every(q_rest)
     for copy in copies:
         copy.wait_recv()
     sums = functools.reduce(jnp.add, [y_buf[d] for d in range(heads)])
@@ -303,51 +366,36 @@
         wide = attn[h].astype(F32)
         grad = (inverse * up[h].astype(F32) - wide * factor).astype(BF16)
         gs[h, OWN] = grad
-        put(normed_ref, h, (wide * inverse).astype(BF16))
+        put(0, h, (wide * inverse).astype(BF16))
         here = jnp.sum(grad.astype(F32) * wide, axis=1, keepdims=True)
         delta[h] = here
-        stat_tile[...] = jnp.where(lane == h + HEADS, here, stat_tile[...])
+        stat_tile[...] = jnp.where(lane == h, here, stat_tile[...])
 
     def gradient_chunk(g):
         heads_of(g, gradient)
         g_flow.own(g)
+        g_flow.far(g)
 
     every(gradient_chunk)
-
-    stats[OWN] = stat_tile[...].T[: 2 * HEADS]
-
-    def stat_copy(k):
-        return pltpu.make_async_remote_copy(
-            src_ref=stats.at[OWN],
-            dst_ref=stats.at[k],
-            send_sem=stat_send.at[k],
-            recv_sem=stat_recv.at[k],
-            device_id=(lax.rem(place - 2**k + BLOCKS, BLOCKS), head),
-            device_id_type=MESH,
-        )
-
-    for k in range(6):
-
-        @pl.when(place >= 2**k)
-        def _():
-            stat_copy(k).start()
+    stats[OWN, 1] = stat_tile[...].T[:HEADS]
+    stat_start(1)
 
     def grad_query(h):
         grad_probs = nt(gs[h, OWN], kv[h, :, 1].reshape(SLOTS * BLOCK, HD))
         held = probs[h].astype(F32)
         dscore = (held * (grad_probs - delta[h]) * row_scale[h]).astype(BF16)
-        put(dq_ref, h, nn(dscore, kv[h, :, 0].reshape(SLOTS * BLOCK, HD)).astype(BF16))
+        put(1, h, nn(dscore, kv[h, :, 0].reshape(SLOTS * BLOCK, HD)).astype(BF16))
 
     def key_probs(h):
         raw = nt(kv[h, OWN, 0], qs[h].reshape(SLOTS * BLOCK, HD))
         parts = []
         for s in range(SLOTS):
-            scores = slot(raw, s) * SCALE2 - stats[s, pl.ds(h, 1), :]
+            scores = slot(raw, s) * SCALE2 - stats[s, 0, pl.ds(h, 1), :]
             if s == OWN:
                 scores = jnp.where(row <= lane, scores, NEG_BIG)
             else:
                 index = place + 2**s
-                live = (pattern_ref[jnp.minimum(index, BLOCKS - 1), s] >= 0) & (index < BLOCKS)
+                live = (pattern_ref[s, jnp.minimum(index, BLOCKS - 1)] >= 0) & (index < BLOCKS)
                 scores = scores + jnp.where(live, 0.0, NEG_BIG).astype(F32)
             parts.append(jnp.exp2(scores).astype(BF16))
         probs_t[h] = jnp.concatenate(parts, axis=1)
@@ -355,14 +403,14 @@
     def grad_keys(h):
         grads = gs[h].reshape(SLOTS * BLOCK, HD)
         held = probs_t[h]
-        put(dv_ref, h, nn(held, grads).astype(BF16))
+        put(3, h, nn(held, grads).astype(BF16))
         raw = nt(kv[h, OWN, 1], grads)
         parts = []
         for s in range(SLOTS):
-            part = slot(raw, s) - stats[s, pl.ds(h + HEADS, 1), :]
+            part = slot(raw, s) - stats[s, 1, pl.ds(h, 1), :]
             parts.append((slot(held, s).astype(F32) * part * SCALE).astype(BF16))
         dscore = jnp.concatenate(parts, axis=1)
-        put(dk_ref, h, nn(dscore, qs[h].reshape(SLOTS * BLOCK, HD)).astype(BF16))
+        put(2, h, nn(dscore, qs[h].reshape(SLOTS * BLOCK, HD)).astype(BF16))
 
     def second_phase(s):
         @pl.when(s < CHUNKS)
@@ -372,11 +420,11 @@
 
         @pl.when(s == 1)
         def _():
-            for k in range(6):
-
-                @pl.when(place + 2**k < BLOCKS)
-                def _():
-                    stat_copy(k).wait_recv()
+            stat_wait(0)
+
+        @pl.when(s == 2)
+        def _():
+            stat_wait(1)
 
         @pl.when((s >= 1) & (s <= CHUNKS))
         def _():
@@ -400,7 +448,36 @@
 
         @pl.when(place >= 2**k)
         def _():
-            stat_copy(k).wait_send()
+            stat_copy(k, 0).wait_send()
+            stat_copy(k, 1).wait_send()
+
+    def stored(h):
+        for a in range(4):
+            store(a, h).wait()
+
+    every(stored, HEADS)
+
+
+def copy_kernel(*refs):
+    sources, targets, held, sem = refs[:4], refs[4:8], refs[8], refs[9]
+    halves = []
+    for a in range(4):
+        for part in range(2):
+            rows = pl.ds(part * BLOCK // 2, BLOCK // 2)
+            here = held.at[a, rows]
+            halves.append(
+                (
+                    pltpu.make_async_copy(sources[a].at[rows], here, sem.at[0, a, part]),
+                    pltpu.make_async_copy(here, targets[a].at[rows], sem.at[1, a, part]),
+                )
+            )
+    for load, _ in halves:
+        load.start()
+    for load, store in halves:
+        load.wait()
+        store.start()
+    for _, store in halves:
+        store.wait()
 
 
 def shards(queries, keys, values, pattern, upstream):
@@ -410,18 +487,20 @@
     tile = (BLOCK, HD)
     dma = pltpu.SemaphoreType.DMA
     anywhere = pl.BlockSpec(memory_space=pl.ANY)
-    return pl.pallas_call(
+    results = pl.pallas_call(
         kernel,
         out_shape=(out,) * 4,
         in_specs=[
             anywhere,
             anywhere,
             anywhere,
-            pl.BlockSpec(memory_space=pltpu.SMEM),
+            anywhere,
             anywhere,
         ],
-        out_specs=[pl.BlockSpec(memory_space=pltpu.VMEM)] * 4,
+        out_specs=[anywhere] * 4,
         scratch_shapes=[
+            pltpu.SMEM((LEVELS + 1, BLOCKS), jnp.int32),
+            pltpu.VMEM((4, HEADS) + tile, BF16),
             pltpu.VMEM((HEADS, SLOTS, 2) + tile, BF16),
             pltpu.VMEM((HEADS, SLOTS) + tile, BF16),
             pltpu.VMEM((HEADS, SLOTS) + tile, BF16),
@@ -432,10 +511,12 @@
             pltpu.VMEM((HEADS, BLOCK, 1), F32),
             pltpu.VMEM((HEADS, BLOCK, 1), F32),
             pltpu.VMEM((BLOCK, BLOCK), F32),
-            pltpu.VMEM((SLOTS, 2 * HEADS, BLOCK), F32),
+            pltpu.VMEM((SLOTS, 2, HEADS, BLOCK), F32),
             pltpu.VMEM(tile, F32),
             pltpu.VMEM(tile, F32),
             pltpu.VMEM((heads, 8, BLOCK), F32),
+            dma,
+            dma((4, HEADS)),
             dma((4, HEADS)),
             dma((CHUNKS, 6)),
             dma((CHUNKS, 6)),
@@ -443,18 +524,26 @@
             dma((CHUNKS, 6)),
             dma((CHUNKS, 6)),
             dma((CHUNKS, 6)),
-            dma((6,)),
-            dma((6,)),
+            dma((6, 2)),
+            dma((6, 2)),
             dma((heads - 1,)),
             dma((heads - 1,)),
         ],
         compiler_params=pltpu.CompilerParams(
-            collective_id=0, has_side_effects=True, vmem_limit_bytes=48 * 1024 * 1024
+            collective_id=0, has_side_effects=True, vmem_limit_bytes=VMEM
         ),
         cost_estimate=pl.CostEstimate(
             flops=2_000_000_000, bytes_accessed=2 * 1024 * 1024, transcendentals=2_000_000
         ),
-    )(queries, keys, values, pattern, upstream)
+    )(queries, keys, values, pattern.T, upstream)
+    return pl.pallas_call(
+        copy_kernel,
+        out_shape=(out,) * 4,
+        in_specs=[anywhere] * 4,
+        out_specs=[anywhere] * 4,
+        scratch_shapes=[pltpu.VMEM((4, tokens, width), BF16), dma((2, 4, 2))],
+        compiler_params=pltpu.CompilerParams(vmem_limit_bytes=VMEM),
+    )(*results)
 
 
 def solution(mesh):

time: 91 us -> 82.3 us (0.904)
  local copies, waits for them, and re-layouts: 7.38 us -> 0 us
  Pallas kernels: 82.2 us -> 81.1 us
    unnamed x13 -> x0, local copies, waits for them, and re-layouts: 7.38 us -> none
    pallas_call x1, Pallas kernels: 82.2 us -> 79 us  [shards(): pl.pallas_call(kernel, out_shape=(out,) * 4, in_specs=[anywhere, anywhere...]
    pallas_call x0 -> x1, Pallas kernels: none -> 2.09 us  [shards(): pl.pallas_call(copy_kernel, out_shape=(out,) * 4, in_specs=[anywhere] * 4...]
where the time goes in v2:
time: 82.3 us; the launch traced here: 81.8 us
  Pallas kernels  81.1 us (99%)
    pallas_call x1, Pallas kernels, shards(): pl.pallas_call(kernel, out_shape=(out,) * 4, in_specs=[anywhere, anywhere...  79 us
    pallas_call x1, Pallas kernels, shards(): pl.pallas_call(copy_kernel, out_shape=(out,) * 4, in_specs=[anywhere] * 4...  2.09 us

profile of v2, /device:TPU:1, one launch (start us, length us, event | category | flops | bytes accessed | tf_op | source)
XLA Modules:
  0.0 81.8 jit_solution(2787890394257272598)
XLA Ops:
  0.6 79.0 %shard_map.84 = (bf16[128,1024]{1,0:T(8,128)(2,1)}, bf16[128,1024]{1,0:T(8,128)(2,1)}, bf16[128,1024]{1,0:T(8,128)(2,1)}, bf16[128,1024]{1,0:T(8,128)(2,1)}) custom-call(bf16[128,1024]{1,0:T(8,128)(2,1)} %q_ref.1, bf16[128,1024]{1,0:T(8,128)(2,1)} %k_ref.1, bf16[128,1024]{1,0:T(8,128)(2,1)} %v_ref.1, s32[8,64]{1,0:T(8,128)} %bitcast.1, bf16[128,1024]{1,0:T(8,128)(2,1)} %u_ref.1), custom_call_target="tpu_custom_call" | custom-call | flops 2000000000 | bytes 2097152 | tf_op jit(solution)/shard_map/pallas_call | solution.py:490
  79.7 2.1 %shard_map.85 = (bf16[128,1024]{1,0:T(8,128)(2,1)}, bf16[128,1024]{1,0:T(8,128)(2,1)}, bf16[128,1024]{1,0:T(8,128)(2,1)}, bf16[128,1024]{1,0:T(8,128)(2,1)}) custom-call(bf16[128,1024]{1,0:T(8,128)(2,1)} %get-tuple-element.8.refs_0_, bf16[128,1024]{1,0:T(8,128)(2,1)} %get-tuple-element.9.refs_1_, bf16[128,1024]{1,0:T(8,128)(2,1)} %get-tuple-element.10.refs_2_, ...), custom_call_target="tpu_custom_call" | custom-call | tf_op jit(solution)/shard_map/pallas_call | solution.py:539

commit v3 on v2

--- a/solution.py
+++ b/solution.py
@@ -20,6 +20,16 @@
 VMEM = 63 * 1024 * 1024
 PER = HEADS // CHUNKS
 LEAD = 1
+LAG_B = 1
+LAG_C = 2
+LAG_QA = 1
+LAG_QB = 2
+G_LAG_P = 1
+KV_RELAYED = 0
+Q_RELAYED = 4
+G_RELAYED = 0
+G_LAG_B = 1
+G_LAG_C = 2
 NEG_BIG = -1e30
 EPSILON = 1e-06
 SCALE = HD**-0.5
@@ -38,9 +48,9 @@
 
 
 class Flow:
-    def __init__(self, buf, send_sem, recv_sem, place, head, mirrored):
+    def __init__(self, buf, send_sem, recv_sem, place, head, mirrored, relayed):
         self.buf, self.send_sem, self.recv_sem = buf, send_sem, recv_sem
-        self.mirrored, self.head = mirrored, head
+        self.mirrored, self.head, self.relayed = mirrored, head, relayed
         self.j = BLOCKS - 1 - place if mirrored else place
         self.z, self.x, self.c = self.j // 8, (self.j // 2) % 4, self.j % 2
 
@@ -68,13 +78,22 @@
     def own(self, g):
         z, x, c = self.z, self.x, self.c
         self.send(z < 7, g, OWN, 3, z + 1, x, c)
+
+    def own_x(self, g):
+        z, x, c = self.z, self.x, self.c
         self.send(x < 3, g, OWN, 1, z, x + 1, c)
         self.send(x < 2, g, OWN, 2, z, x + 2, c)
         self.send(c == 0, g, OWN, 0, z, x, 1)
 
+    def direct(self, g):
+        return ((self.z == 1) | (self.z == 3)) & (g >= self.relayed)
+
+    def relay(self, g):
+        z = self.z
+        return (z == 2) | (z == 4) | (((z == 3) | (z == 5)) & (g < self.relayed))
+
     def far(self, g):
-        z, x, c = self.z, self.x, self.c
-        self.send((z == 1) | (z == 3), g, OWN, 5, z + 4, x, c)
+        self.send(self.direct(g), g, OWN, 5, self.z + 4, self.x, self.c)
 
     def stage_a(self, g):
         z, x, c = self.z, self.x, self.c
@@ -92,7 +111,7 @@
         @pl.when(z >= 2)
         def _():
             self.copy(g, OWN, 4).wait_recv()
-            self.send((z == 2) | (z == 4), g, 4, 5, z + 2, x, c)
+            self.send(self.relay(g), g, 4, 5, z + 2, x, c)
 
         @pl.when(self.j >= 2)
         def _():
@@ -114,7 +133,7 @@
             ((x < 2) | (z >= 1), 2),
             (z < 7, 3),
             ((z >= 1) & (z < 7), 4),
-            ((z >= 1) & (z <= 4), 5),
+            (self.direct(g) | self.relay(g), 5),
         ):
 
             @pl.when(condition)
@@ -203,9 +222,9 @@
     for copy in loads:
         copy.start()
 
-    kv_flow = Flow(kv, kv_send, kv_recv, place, head, False)
-    q_flow = Flow(qs, q_send, q_recv, place, head, True)
-    g_flow = Flow(gs, g_send, g_recv, place, head, True)
+    kv_flow = Flow(kv, kv_send, kv_recv, place, head, False, KV_RELAYED)
+    q_flow = Flow(qs, q_send, q_recv, place, head, True, Q_RELAYED)
+    g_flow = Flow(gs, g_send, g_recv, place, head, True, G_RELAYED)
     for flow in (kv_flow, q_flow, g_flow):
         flow.clear()
     for k in range(6):
@@ -281,30 +300,36 @@
 
         lax.fori_loop(0, PER, step, 0)
 
+    def at(step, body):
+        @pl.when((step >= 0) & (step < CHUNKS))
+        def _():
+            body(step)
+
+    def kv_done(g):
+        kv_flow.stage_c(g)
+        heads_of(g, forward)
+
+    def q_send_chunk(g):
+        q_flow.own(g)
+        q_flow.far(g)
+
     def first_phase(s):
-        @pl.when(s < CHUNKS)
-        def _():
-            kv_flow.stage_a(s)
+        at(s, kv_flow.stage_a)
 
         @pl.when(s < CHUNKS - LEAD)
         def _():
             kv_send_chunk(s + LEAD)
 
-        @pl.when((s >= 1) & (s <= CHUNKS))
-        def _():
-            kv_flow.stage_b(s - 1)
-
-        @pl.when(s < CHUNKS)
-        def _():
-            q_flow.own(s)
-
-        @pl.when(s >= 2)
-        def _():
-            q_flow.stage_a(s - 2)
-            kv_flow.stage_c(s - 2)
-            heads_of(s - 2, forward)
-
-    every(first_phase, CHUNKS + 2)
+        at(s, kv_flow.own_x)
+
+        at(s - LAG_B, kv_flow.stage_b)
+        at(s, q_send_chunk)
+        at(s, q_flow.own_x)
+        at(s - LAG_QA, q_flow.stage_a)
+        at(s - LAG_QB, q_flow.stage_b)
+        at(s - LAG_C, kv_done)
+
+    every(first_phase, CHUNKS + max(LAG_C, LAG_QB))
 
     stats[OWN, 0] = stat_tile[...].T[:HEADS]
 
@@ -350,11 +375,6 @@
         copies.append(copy)
     stat_start(0)
 
-    def q_rest(g):
-        q_flow.far(g)
-        q_flow.stage_b(g)
-
-    every(q_rest)
     for copy in copies:
         copy.wait_recv()
     sums = functools.reduce(jnp.add, [y_buf[d] for d in range(heads)])
@@ -371,10 +391,13 @@
         delta[h] = here
         stat_tile[...] = jnp.where(lane == h, here, stat_tile[...])
 
+    def g_send(g):
+        g_flow.own(g)
+        g_flow.own_x(g)
+        g_flow.far(g)
+
     def gradient_chunk(g):
         heads_of(g, gradient)
-        g_flow.own(g)
-        g_flow.far(g)
 
     every(gradient_chunk)
     stats[OWN, 1] = stat_tile[...].T[:HEADS]
@@ -412,32 +435,35 @@
         dscore = jnp.concatenate(parts, axis=1)
         put(2, h, nn(dscore, qs[h].reshape(SLOTS * BLOCK, HD)).astype(BF16))
 
+    every(g_send)
+
+    def key_probs_chunk(g):
+        @pl.when(g == 0)
+        def _():
+            stat_wait(0)
+
+        q_flow.stage_c(g)
+        heads_of(g, key_probs)
+
+    def key_grads(g):
+        @pl.when(g == 0)
+        def _():
+            stat_wait(1)
+
+        g_flow.stage_c(g)
+        heads_of(g, grad_keys)
+
+    def grad_query_chunk(g):
+        heads_of(g, grad_query)
+
     def second_phase(s):
-        @pl.when(s < CHUNKS)
-        def _():
-            heads_of(s, grad_query)
-            g_flow.stage_a(s)
-
-        @pl.when(s == 1)
-        def _():
-            stat_wait(0)
-
-        @pl.when(s == 2)
-        def _():
-            stat_wait(1)
-
-        @pl.when((s >= 1) & (s <= CHUNKS))
-        def _():
-            g_flow.stage_b(s - 1)
-            q_flow.stage_c(s - 1)
-            heads_of(s - 1, key_probs)
-
-        @pl.when(s >= 2)
-        def _():
-            g_flow.stage_c(s - 2)
-            heads_of(s - 2, grad_keys)
-
-    every(second_phase, CHUNKS + 2)
+        at(s, grad_query_chunk)
+        at(s, g_flow.stage_a)
+        at(s - G_LAG_B, g_flow.stage_b)
+        at(s - G_LAG_P, key_probs_chunk)
+        at(s - G_LAG_C, key_grads)
+
+    every(second_phase, CHUNKS + G_LAG_C)
 
     every(kv_flow.drain)
     every(q_flow.drain)

time: 82.3 us -> 81.2 us (0.987)
  no operation moved by 1% of the time
where the time goes in v3:
time: 81.2 us; the launch traced here: 81 us
  Pallas kernels  80.4 us (99%)
    pallas_call x1, Pallas kernels, shards(): pl.pallas_call(kernel, out_shape=(out,) * 4, in_specs=[anywhere, anywhere...  78.3 us
    pallas_call x1, Pallas kernels, shards(): pl.pallas_call(copy_kernel, out_shape=(out,) * 4, in_specs=[anywhere] * 4...  2.09 us

profile of v3, /device:TPU:1, one launch (start us, length us, event | category | flops | bytes accessed | tf_op | source)
XLA Modules:
  0.0 81.0 jit_solution(3799521127021078048)
XLA Ops:
  0.6 78.3 %shard_map.84 = (bf16[128,1024]{1,0:T(8,128)(2,1)}, bf16[128,1024]{1,0:T(8,128)(2,1)}, bf16[128,1024]{1,0:T(8,128)(2,1)}, bf16[128,1024]{1,0:T(8,128)(2,1)}) custom-call(bf16[128,1024]{1,0:T(8,128)(2,1)} %q_ref.1, bf16[128,1024]{1,0:T(8,128)(2,1)} %k_ref.1, bf16[128,1024]{1,0:T(8,128)(2,1)} %v_ref.1, s32[8,64]{1,0:T(8,128)} %bitcast.1, bf16[128,1024]{1,0:T(8,128)(2,1)} %u_ref.1), custom_call_target="tpu_custom_call" | custom-call | flops 2000000000 | bytes 2097152 | tf_op jit(solution)/shard_map/pallas_call | solution.py:516
  78.9 2.1 %shard_map.85 = (bf16[128,1024]{1,0:T(8,128)(2,1)}, bf16[128,1024]{1,0:T(8,128)(2,1)}, bf16[128,1024]{1,0:T(8,128)(2,1)}, bf16[128,1024]{1,0:T(8,128)(2,1)}) custom-call(bf16[128,1024]{1,0:T(8,128)(2,1)} %get-tuple-element.8.refs_0_, bf16[128,1024]{1,0:T(8,128)(2,1)} %get-tuple-element.9.refs_1_, bf16[128,1024]{1,0:T(8,128)(2,1)} %get-tuple-element.10.refs_2_, ...), custom_call_target="tpu_custom_call" | custom-call | tf_op jit(solution)/shard_map/pallas_call | solution.py:565

commit v4 on v3

--- a/solution.py
+++ b/solution.py
@@ -236,7 +236,9 @@
     squares[...] = jnp.zeros(squares.shape, F32)
     crosses[...] = jnp.zeros(crosses.shape, F32)
     stat_tile[...] = jnp.zeros(stat_tile.shape, F32)
-    for copy in loads:
+    first = [copy for i, copy in enumerate(loads[1:]) if i % 4 < 2]
+    rest = loads[:1] + [copy for i, copy in enumerate(loads[1:]) if i % 4 >= 2]
+    for copy in first:
         copy.wait()
     pl.semaphore_wait(barrier, len(partners))
 
@@ -252,6 +254,8 @@
         kv_flow.far(g)
 
     every(kv_send_chunk, LEAD)
+    for copy in rest:
+        copy.wait()
 
     row = lax.broadcasted_iota(jnp.int32, (BLOCK, BLOCK), 0)
     lane = lax.broadcasted_iota(jnp.int32, (BLOCK, BLOCK), 1)
@@ -486,23 +490,23 @@
 
 def copy_kernel(*refs):
     sources, targets, held, sem = refs[:4], refs[4:8], refs[8], refs[9]
-    halves = []
+    pieces = []
     for a in range(4):
-        for part in range(2):
-            rows = pl.ds(part * BLOCK // 2, BLOCK // 2)
+        for part in range(4):
+            rows = pl.ds(part * BLOCK // 4, BLOCK // 4)
             here = held.at[a, rows]
-            halves.append(
+            pieces.append(
                 (
                     pltpu.make_async_copy(sources[a].at[rows], here, sem.at[0, a, part]),
                     pltpu.make_async_copy(here, targets[a].at[rows], sem.at[1, a, part]),
                 )
             )
-    for load, _ in halves:
+    for load, _ in pieces:
         load.start()
-    for load, store in halves:
+    for load, store in pieces:
         load.wait()
         store.start()
-    for _, store in halves:
+    for _, store in pieces:
         store.wait()
 
 
@@ -567,7 +571,7 @@
         out_shape=(out,) * 4,
         in_specs=[anywhere] * 4,
         out_specs=[anywhere] * 4,
-        scratch_shapes=[pltpu.VMEM((4, tokens, width), BF16), dma((2, 4, 2))],
+        scratch_shapes=[pltpu.VMEM((4, tokens, width), BF16), dma((2, 4, 4))],
         compiler_params=pltpu.CompilerParams(vmem_limit_bytes=VMEM),
     )(*results)
 

time: 81.2 us -> 81.3 us (level)
  no operation moved by 1% of the time
where the time goes in v4:
time: 81.3 us; the launch traced here: 81.1 us
  Pallas kernels  80.4 us (99%)
    pallas_call x1, Pallas kernels, shards(): pl.pallas_call(kernel, out_shape=(out,) * 4, in_specs=[anywhere, anywhere...  78.3 us
    pallas_call x1, Pallas kernels, shards(): pl.pallas_call(copy_kernel, out_shape=(out,) * 4, in_specs=[anywhere] * 4...  2.16 us

profile of v4, /device:TPU:1, one launch (start us, length us, event | category | flops | bytes accessed | tf_op | source)
XLA Modules:
  0.0 81.1 jit_solution(15444869415179221904)
XLA Ops:
  0.6 78.3 %shard_map.84 = (bf16[128,1024]{1,0:T(8,128)(2,1)}, bf16[128,1024]{1,0:T(8,128)(2,1)}, bf16[128,1024]{1,0:T(8,128)(2,1)}, bf16[128,1024]{1,0:T(8,128)(2,1)}) custom-call(bf16[128,1024]{1,0:T(8,128)(2,1)} %q_ref.1, bf16[128,1024]{1,0:T(8,128)(2,1)} %k_ref.1, bf16[128,1024]{1,0:T(8,128)(2,1)} %v_ref.1, s32[8,64]{1,0:T(8,128)} %bitcast.1, bf16[128,1024]{1,0:T(8,128)(2,1)} %u_ref.1), custom_call_target="tpu_custom_call" | custom-call | flops 2000000000 | bytes 2097152 | tf_op jit(solution)/shard_map/pallas_call | solution.py:520
  78.9 2.2 %shard_map.85 = (bf16[128,1024]{1,0:T(8,128)(2,1)}, bf16[128,1024]{1,0:T(8,128)(2,1)}, bf16[128,1024]{1,0:T(8,128)(2,1)}, bf16[128,1024]{1,0:T(8,128)(2,1)}) custom-call(bf16[128,1024]{1,0:T(8,128)(2,1)} %get-tuple-element.8.refs_0_, bf16[128,1024]{1,0:T(8,128)(2,1)} %get-tuple-element.9.refs_1_, bf16[128,1024]{1,0:T(8,128)(2,1)} %get-tuple-element.10.refs_2_, ...), custom_call_target="tpu_custom_call" | custom-call | tf_op jit(solution)/shard_map/pallas_call | solution.py:569
